TPU v7x, 256 devices: a whole 4x4x8 slice. The times are simulated.
256 devices in a mesh: samp: 8 (over z_hi, core), seq: 32 (over x, y, z_lo).
Axes of the slice: x: 4, y: 4, z: 8 (z_hi: 4, z_lo: 2; z = z_hi * 2 + z_lo), core: 2. Of those that a mesh axis runs over, the one named last changes fastest.
Arguments:
- atom_act: bfloat16 [16, 12288, 128], P('samp', 'seq'), may hold values from -6 to 6
- atom_gain: float32 [128], replicated, may hold values from 0.25 to 1.75
- atom_query: bfloat16 [128, 128], replicated, may hold values from -0.5 to 0.5
- atom_keyval: bfloat16 [128, 256], replicated, may hold values from -0.5 to 0.5
- atom_output: bfloat16 [128, 128], replicated, may hold values from -0.5 to 0.5
- atom_bias: bfloat16 [4, 384, 32, 128], P(None, 'seq'), may hold values from -4 to 298
- key_range: int32 [384, 2], P('seq'), may hold values from 0 to 12288, as said below
- atom_token: int32 [12288], P('seq'), may hold values from 0 to 1535, as said below
- token_counts: int32 [1536], P('seq'), may hold values from 1 to 15, as said below
- gather_weight: bfloat16 [128, 768], replicated, may hold values from -0.5 to 0.5
- token_gain: float32 [768], replicated, may hold values from 0.25 to 1.75
- token_query: bfloat16 [768, 768], replicated, may hold values from -0.21875 to 0.21875
- token_keyval: bfloat16 [768, 1536], replicated, may hold values from -0.21875 to 0.21875
- token_output: bfloat16 [768, 768], replicated, may hold values from -0.21875 to 0.21875
- pair_bias: bfloat16 [16, 1536, 1536], P('samp', 'seq'), may hold values from -4 to 298
- trans_gain: float32 [768], replicated, may hold values from 0.25 to 1.75
- trans_gate_up: bfloat16 [768, 3072], replicated, may hold values from -0.21875 to 0.21875
- trans_down: bfloat16 [1536, 768], replicated, may hold values from -0.15625 to 0.15625
- back_weight: bfloat16 [768, 128], replicated, may hold values from -0.21875 to 0.21875
Outputs:
- atom_out: bfloat16 [16, 12288, 128], P('samp', 'seq')
- token_out: bfloat16 [16, 1536, 768], P('samp', 'seq')
Inputs may be any that keep to these rules, and one draw needn't show every extreme that they name: max(0, 32 * b - 48) <= key_range[b, 0] <= 32 * b and 32 * b + 32 <= key_range[b, 1] <= min(12288, 32 * b + 80). atom_token never falls along the atoms; atom a belongs to token a // 8 or a // 8 - 1. token_counts[t] is the number of atoms a with atom_token[a] = t.
All inputs are finite; a program needn't handle non-finite values.
Results may differ from a plain program's by a relative error of at most 0.025.
Values may be sent and summed in bfloat16 or wider, within the bound.
No kernel may reach another device: no remote copies, remote signals or barrier semaphores. Data moves between devices by JAX's collectives and lax.ppermute only.
A program may use at most 128 MiB of HBM per device.

v0:
```python
import math
import jax
import jax.numpy as jnp
from jax import lax
from jax.sharding import PartitionSpec as P

AH = 4
HEADS = 16
WQ = 32
WK = 128
EDGE = 48
EPSILON = 1e-05
NEGATIVE = -1e30


def extended(cells, sides, width):
    for axis, dim in sides:
        count = lax.axis_size(axis)
        ends = count - 1
        head = lax.slice_in_dim(cells, 0, width, axis=dim)
        tail = lax.slice_in_dim(cells, cells.shape[dim] - width, cells.shape[dim], axis=dim)
        cells = jnp.concatenate(
            [
                lax.ppermute(tail, axis, [(i, (i + 1) % count) for i in range(ends)]),
                cells,
                lax.ppermute(head, axis, [((i + 1) % count, i) for i in range(ends)]),
            ],
            axis=dim,
        )
    return cells


def passed_along(value, axis, by):
    devices = lax.axis_size(axis)
    pairs = [(i, i + by) for i in range(devices) if 0 <= i + by < devices]
    return lax.ppermute(value, axis, pairs)


def layer_norm(values, gain_vector):
    widened = values.astype(jnp.float32)
    centred = widened - jnp.mean(widened, axis=-1, keepdims=True)
    variance = jnp.mean(centred * centred, axis=-1, keepdims=True)
    return (centred * lax.rsqrt(variance + EPSILON) * gain_vector).astype(jnp.bfloat16)


def softmax_rows(scores):
    maxima = jnp.max(scores, axis=-1, keepdims=True)
    exponent = jnp.exp(scores - maxima)
    return exponent / jnp.sum(exponent, axis=-1, keepdims=True)


def project(values, weight):
    return jnp.einsum("sac,cd->sad", values, weight, preferred_element_type=jnp.float32)


def make_attend(query_heads, bias_rows, head_count, head_size, score_scale):

    def attend(running, keyval_piece, first_key):
        best_score, row_total, value_sum = running
        sample_count = keyval_piece.shape[0]
        piece_rows = keyval_piece.shape[1]
        key_heads = keyval_piece[:, :, 0].reshape(sample_count, piece_rows, head_count, head_size)
        value_heads = keyval_piece[:, :, 1].reshape(sample_count, piece_rows, head_count, head_size)
        piece_scores = jnp.einsum(
            "sqhd,skhd->shqk", query_heads, key_heads, preferred_element_type=jnp.float32
        )
        piece_scores = piece_scores * score_scale + bias_rows.astype(jnp.float32)[None]
        new_best = jnp.maximum(best_score, jnp.max(piece_scores, axis=-1))
        exponent = jnp.exp(piece_scores - new_best[..., None])
        row_total = jnp.sum(exponent, axis=-1)
        value_sum = jnp.einsum(
            "shqk,skhd->shqd",
            exponent.astype(jnp.bfloat16),
            value_heads,
            preferred_element_type=jnp.float32,
        )
        return (new_best, row_total, value_sum)

    return attend


def initial_state(sample_count, head_count, token_rows, head_size):
    return (
        jnp.full((sample_count, head_count, token_rows), NEGATIVE, jnp.float32),
        jnp.zeros((sample_count, head_count, token_rows), jnp.float32),
        jnp.zeros((sample_count, head_count, token_rows, head_size), jnp.float32),
    )


def per_device(
    atom_act,
    atom_gain,
    atom_query,
    atom_keyval,
    atom_output,
    atom_bias,
    key_range,
    atom_token,
    token_counts,
    gather_weight,
    token_gain,
    token_query,
    token_keyval,
    token_output,
    pair_bias,
    trans_gain,
    trans_gate_up,
    trans_down,
    back_weight,
):
    samples, atom_rows, channels = atom_act.shape
    windows = atom_rows // WQ
    head_width = channels // AH
    atom_scale = 1.0 / math.sqrt(head_width)
    normed = layer_norm(atom_act, atom_gain)
    queries = project(normed, atom_query).astype(jnp.bfloat16)
    keyvals = project(normed, atom_keyval).astype(jnp.bfloat16)
    padded = extended(keyvals, (("seq", 1),), EDGE)
    blocks = padded.reshape(samples, windows + 2 * EDGE // WQ, WQ, 2 * channels)
    window_keys = jnp.concatenate(
        [blocks[:, shift_at : shift_at + windows] for shift_at in range(WK // WQ)], axis=2
    )
    key_part = window_keys[..., :channels].reshape(samples, windows, WK, AH, head_width)
    value_part = window_keys[..., channels:].reshape(samples, windows, WK, AH, head_width)
    query_part = queries.reshape(samples, windows, WQ, AH, head_width)
    scores = jnp.einsum(
        "swqhd,swkhd->shwqk", query_part, key_part, preferred_element_type=jnp.float32
    )
    scores = scores * atom_scale + atom_bias.astype(jnp.float32)[None]
    window_base = lax.axis_index("seq") * windows + jnp.arange(windows, dtype=jnp.int32)
    position = WQ * window_base[:, None] - EDGE + jnp.arange(WK, dtype=jnp.int32)[None, :]
    key_valid = (position >= key_range[:, 0:1]) & (position < key_range[:, 1:2])
    scores = jnp.where(key_valid[None, None, :, None, :], scores, NEGATIVE)
    weights = softmax_rows(scores).astype(jnp.bfloat16)
    attended = jnp.einsum(
        "shwqk,swkhd->swqhd", weights, value_part, preferred_element_type=jnp.float32
    )
    attended = attended.astype(jnp.bfloat16).reshape(samples, atom_rows, channels)
    atom_mid = (atom_act.astype(jnp.float32) + project(attended, atom_output)).astype(jnp.bfloat16)
    token_rows = token_counts.shape[0]
    first_token = lax.axis_index("seq") * token_rows
    token_slot = atom_token - first_token
    hidden_atoms = jax.nn.relu(project(atom_mid, gather_weight)).astype(jnp.bfloat16)
    own_table = (token_slot[:, None] == jnp.arange(token_rows, dtype=jnp.int32)[None, :]).astype(
        jnp.bfloat16
    )
    own_sums = jnp.einsum(
        "at,sad->std", own_table, hidden_atoms, preferred_element_type=jnp.float32
    )
    before_table = (token_slot == -1).astype(jnp.bfloat16)
    before_sum = jnp.einsum(
        "a,sad->sd", before_table, hidden_atoms, preferred_element_type=jnp.float32
    )
    arrived = passed_along(before_sum, "seq", -1)
    own_sums = own_sums.at[:, token_rows - 1].add(arrived)
    token_act = (own_sums / token_counts.astype(jnp.float32)[None, :, None]).astype(jnp.bfloat16)
    token_norm = layer_norm(token_act, token_gain)
    token_queries = project(token_norm, token_query).astype(jnp.bfloat16)
    model_width = token_norm.shape[-1]
    head_size = model_width // HEADS
    score_scale = 1.0 / math.sqrt(head_size)
    all_bias = lax.all_gather(pair_bias, "samp", axis=0, tiled=True)
    query_heads = token_queries.reshape(samples, token_rows, HEADS, head_size)
    attend = make_attend(query_heads, all_bias, HEADS, head_size, score_scale)
    initial = initial_state(samples, HEADS, token_rows, head_size)
    token_keyvals = (
        project(token_norm, token_keyval)
        .astype(jnp.bfloat16)
        .reshape(samples, token_rows, 2, model_width)
    )
    best_score, row_total, value_sum = attend(
        initial, lax.all_gather(token_keyvals, "seq", axis=1, tiled=True), jnp.int32(0)
    )
    attended_tokens = (value_sum / row_total[..., None]).astype(jnp.bfloat16)
    merged = jnp.einsum(
        "shqd,hde->sqe",
        attended_tokens,
        token_output.reshape(HEADS, head_size, model_width),
        preferred_element_type=jnp.float32,
    )
    token_mid = (token_act.astype(jnp.float32) + merged).astype(jnp.bfloat16)
    trans_norm = layer_norm(token_mid, trans_gain)
    gate_up = project(trans_norm, trans_gate_up)
    hidden_width = trans_down.shape[0]
    hidden = (jax.nn.silu(gate_up[..., :hidden_width]) * gate_up[..., hidden_width:]).astype(
        jnp.bfloat16
    )
    token_out = (token_mid.astype(jnp.float32) + project(hidden, trans_down)).astype(jnp.bfloat16)
    back_rows = project(token_out, back_weight).astype(jnp.bfloat16)
    previous = passed_along(back_rows[:, token_rows - 1], "seq", 1)
    back_table = jnp.concatenate([previous[:, None], back_rows], axis=1)
    lookup = (
        (token_slot + 1)[:, None] == jnp.arange(token_rows + 1, dtype=jnp.int32)[None, :]
    ).astype(jnp.bfloat16)
    gathered_back = jnp.einsum(
        "at,stc->sac", lookup, back_table, preferred_element_type=jnp.float32
    )
    atom_out = (atom_mid.astype(jnp.float32) + gathered_back).astype(jnp.bfloat16)
    return (atom_out, token_out)


def solution(mesh):
    placed = (
        P("samp", "seq", None),
        P(),
        P(),
        P(),
        P(),
        P(None, "seq", None, None),
        P("seq", None),
        P("seq"),
        P("seq"),
        P(),
        P(),
        P(),
        P(),
        P(),
        P("samp", "seq", None),
        P(),
        P(),
        P(),
        P(),
    )
    return jax.shard_map(
        per_device,
        mesh=mesh,
        in_specs=placed,
        out_specs=(P("samp", "seq", None), P("samp", "seq", None)),
        check_vma=False,
    )
```

profile of v0, /device:TPU:6, one launch (start us, length us, event | category | flops | bytes accessed | tf_op | source)
XLA Modules:
  0.0 380.0 jit_solution(8645867233082741902)
XLA Ops:
  7.2 1.3 convert_reduce_fusion
  8.5 1.2 fusion.52
  9.7 1.3 convolution_convert_fusion.1
  11.1 6.5 %collective-permute-start.1 = (bf16[2,48,256]{2,1,0:T(8,128)(2,1)S(1)}, bf16[2,48,256]{2,1,0:T(8,128)(2,1)S(1)}, u32[]{:S(2)}, u32[]{:S(2)}) collective-permute-start(bf16[2,48,256]{2,1,0:T(8,128)(2,1)S(1)} %get-tuple-element.27), channel_id=1, source_target_pairs={{1,0},{2,1},{3,2},{4,3},{5,4},{6,5},{7,6},{8,7},{9,8},{10,9},{11,1... | collective-permute-start | bytes 147464 | tf_op jit(solution)/shard_map/ppermute | solution.py:26
  17.7 1.9 collective-permute-start
  19.7 1.3 convolution_convert_fusion.2
  21.8 1.2 broadcast_compare_fusion
  23.0 1.2 reshape.168
  27.7 2.4 copy.78
  30.1 1.5 copy.77
  31.6 1.6 copy.76
  33.1 1.5 copy.75
  34.7 5.0 %pad_maximum_fusion = bf16[2,12,128,256]{2,3,1,0:T(8,128)(2,1)S(1)} fusion(bf16[2,12,32,256]{2,3,1,0:T(8,128)(2,1)} %copy.78, bf16[2,12,32,256]{2,3,1,0:T(8,128)(2,1)} %copy.77, bf16[2,12,32,256]{2,3,1,0:T(8,128)(2,1)} %copy.76, bf16[2,12,32,256]{2,3,1,0:T(8,128)(2,1)} %copy.75), kind=kLoop, calls=%fused_computation.19 | loop fusion | flops 6291456 | bytes 3145728 | tf_op jit(solution)/shard_map/concatenate | solution.py:120
  39.7 1.3 fusion.96
  41.0 3.2 fusion.99
  44.2 3.2 fusion.20
  47.4 1.5 copy.62
  50.4 1.4 maximum_convert_fusion
  52.1 6.6 %collective-permute-start.2 = (f32[2,768]{1,0:T(2,128)S(1)}, f32[2,768]{1,0:T(2,128)S(1)}, u32[]{:S(2)}, u32[]{:S(2)}) collective-permute-start(f32[2,768]{1,0:T(2,128)S(1)} %bitcast.103), channel_id=1, source_target_pairs={{1,0},{2,1},{3,2},{4,3},{5,4},{6,5},{7,6},{8,7},{9,8},{10,9},{11,1... | collective-permute-start | bytes 18440 | tf_op jit(solution)/shard_map/ppermute | solution.py:36
  62.4 1.6 fusion.33
  64.5 4.5 %convert_element_type.104 = f32[16,48,1536]{2,1,0:T(8,128)} convert(bf16[16,48,1536]{2,1,0:T(8,128)(2,1)} %all-gather.5.cloned.1.call-done) | non-fusion elementwise | flops 1179648 | bytes 7077888 | tf_op jit(solution)/shard_map/convert_element_type | solution.py:67
  69.0 208.9 %all-gather.3.cloned.1.call-done = bf16[2,1536,2,768]{3,2,0,1:T(2,128)(2,1)} async-done(((bf16[2,48,2,768]{3,2,0,1:T(2,128)(2,1)}), bf16[2,1536,2,768]{3,2,0,1:T(2,128)(2,1)}) %all-gather.3.cloned.1.call-update) | async-done | bytes 9437200 | tf_op jit(solution)/shard_map/all_gather | solution.py:172
  277.9 19.5 %fusion.95 = (bf16[2,1536,1,768]{3,2,0,1:T(2,128)(2,1)}, bf16[2,1536,1,768]{3,2,0,1:T(2,128)(2,1)}) fusion(bf16[2,1536,2,768]{3,2,0,1:T(2,128)(2,1)} %all-gather.3.cloned.1.call-done), kind=kLoop, calls=%fused_computation.113 | loop fusion | bytes 18874368 | tf_op jit(solution)/shard_map/slice | solution.py:62
  297.5 22.4 %copy.79 = bf16[2,1536,1,768]{1,3,0,2:T(8,128)(2,1)} copy(bf16[2,1536,1,768]{3,2,0,1:T(2,128)(2,1)} %get-tuple-element.19) | data formatting | bytes 9437184
  319.9 22.4 %copy.65 = bf16[2,1536,1,768]{1,3,0,2:T(8,128)(2,1)} copy(bf16[2,1536,1,768]{3,2,0,1:T(2,128)(2,1)} %get-tuple-element.18) | data formatting | bytes 9437184 | tf_op jit(solution)/shard_map/slice | solution.py:62
  342.3 5.1 %fusion.1 = (f32[2,16,48]{2,1,0:T(8,128)S(1)}, f32[2,16,48,1536]{3,2,1,0:T(8,128)S(1)}) fusion(f32[16,48,1536]{2,1,0:T(8,128)} %convert_element_type.104, bf16[2,1536,16,48]{1,3,2,0:T(8,128)(2,1)} %bitcast.96, bf16[2,48,16,48]{3,2,1,0:T(8,128)(2,1)S(1)} %reshape.172), kind=kOutput, calls=%fused_computation.3 | convolution fusion | flops 233568768 | bytes 19027968 | tf_op jit(solution)/shard_map/sqhd,skhd->shqk/dot_general | solution.py:64
  347.5 2.1 fusion.2
  349.6 1.4 copy-done.2
  351.0 8.0 %fusion.100 = (f32[2,48]{1,0:T(2,128)S(1)}, f32[2,48,768]{2,1,0:T(8,128)S(1)}) fusion(bf16[16,48,768,1]{2,1,0,3:T(8,128)(2,1)S(1)} %bitcast.100, bf16[2,1536,16,48]{1,3,2,0:T(8,128)(2,1)} %bitcast.97, f32[2,16,48,1536]{3,2,1,0:T(8,128)} %copy-done.2, f32[2,16,48]{2,1,0:T(8,128)S(1)} %broadcast_maximum_fusion, f32[16,48,1536]{2,1,0:T(8,128)} %convert_element_type.104, ...), kind=kOutput, calls=%fused_computation.118 | convolution fusion | flops 349691808 | bytes 20509056 | tf_op jit(solution)/shard_map/shqd,hde->sqe/dot_general | solution.py:175
  359.2 3.4 fusion.6
  363.8 1.9 collective-permute-start.3
  365.7 6.5 %collective-permute-done.3 = bf16[2,128]{1,0:T(2,128)(2,1)S(1)} collective-permute-done((bf16[2,128]{1,0:T(2,128)(2,1)S(1)}, bf16[2,128]{1,0:T(2,128)(2,1)S(1)}, u32[]{:S(2)}, u32[]{:S(2)}) %collective-permute-start.3) | collective-permute-done | bytes 544 | tf_op jit(solution)/shard_map/ppermute | solution.py:36
  (75 shorter events, 12.4 us)
Async XLA Ops:
  7.2 53.6 %copy-start = (bf16[768,1536]{1,0:T(8,128)(2,1)S(1)}, bf16[768,1536]{1,0:T(8,128)(2,1)}, u32[]{:S(2)}) copy-start(bf16[768,1536]{1,0:T(8,128)(2,1)} %param.33) | copy-start | bytes 7077892
  7.2 17.1 %copy-start.6 = (bf16[4,12,32,128]{3,2,1,0:T(8,128)(2,1)S(1)}, bf16[4,12,32,128]{3,2,1,0:T(8,128)(2,1)}, u32[]{:S(2)}) copy-start(bf16[4,12,32,128]{3,2,1,0:T(8,128)(2,1)} %param.26) | copy-start | bytes 1179652
  7.2 57.3 %all-gather.5.cloned.1.call-start = ((), (), s32[]{:S(2)}) async-start(), calls=%async_computation.1 | async-start | bytes 2654208 | tf_op jit(solution)/shard_map/all_gather | solution.py:162
  11.1 15.5 %collective-permute-start.1 = (bf16[2,48,256]{2,1,0:T(8,128)(2,1)S(1)}, bf16[2,48,256]{2,1,0:T(8,128)(2,1)S(1)}, u32[]{:S(2)}, u32[]{:S(2)}) collective-permute-start(bf16[2,48,256]{2,1,0:T(8,128)(2,1)S(1)} %get-tuple-element.27), channel_id=1, source_target_pairs={{1,0},{2,1},{3,2},{4,3},{5,4},{6,5},{7,6},{8,7},{9,8},{10,9},{11,1... | collective-permute-start | bytes 147464 | tf_op jit(solution)/shard_map/ppermute | solution.py:26
  17.7 9.0 %collective-permute-start = (bf16[2,48,256]{2,1,0:T(8,128)(2,1)S(1)}, bf16[2,48,256]{2,1,0:T(8,128)(2,1)S(1)}, u32[]{:S(2)}, u32[]{:S(2)}) collective-permute-start(bf16[2,48,256]{2,1,0:T(8,128)(2,1)S(1)} %get-tuple-element.26), channel_id=1, source_target_pairs={{0,1},{1,2},{2,3},{3,4},{4,5},{5,6},{6,7},{7,8},{8,9},{9,10},{10,1... | collective-permute-start | bytes 147464 | tf_op jit(solution)/shard_map/ppermute | solution.py:24
  19.6 258.3 %all-gather.3.cloned.1.call-start = ((), (), s32[]{:S(2)}) async-start(), calls=%async_computation | async-start | bytes 9732096 | tf_op jit(solution)/shard_map/all_gather | solution.py:172
  39.7 1.3 copy-start.5
  47.4 2.0 copy-start.3
  50.4 10.4 %copy-start.10 = (f32[768]{0:T(1024)S(1)}, f32[768]{0:T(1024)}, u32[]{:S(2)}) copy-start(f32[768]{0:T(1024)} %param.31) | copy-start | bytes 9220
  52.1 8.0 %collective-permute-start.2 = (f32[2,768]{1,0:T(2,128)S(1)}, f32[2,768]{1,0:T(2,128)S(1)}, u32[]{:S(2)}, u32[]{:S(2)}) collective-permute-start(f32[2,768]{1,0:T(2,128)S(1)} %bitcast.103), channel_id=1, source_target_pairs={{1,0},{2,1},{3,2},{4,3},{5,4},{6,5},{7,6},{8,7},{9,8},{10,9},{11,1... | collective-permute-start | bytes 18440 | tf_op jit(solution)/shard_map/ppermute | solution.py:36
  342.3 5.2 %slice-start = ((s8[4718592]{0:T(1024)(128)(4,1)}), s8[4194304]{0:T(1024)(128)(4,1)S(1)}, s32[]{:S(2)}) async-start(s8[4718592]{0:T(1024)(128)(4,1)} %bitcast.94), calls=%async_computation.2 | async-start | bytes 8388608
  342.3 5.2 %slice-start.1 = ((s8[4718592]{0:T(1024)(128)(4,1)}), s8[524288]{0:T(1024)(128)(4,1)S(1)}, s32[]{:S(2)}) async-start(s8[4718592]{0:T(1024)(128)(4,1)} %bitcast.94), calls=%async_computation.3 | async-start | bytes 1048576
  347.4 3.6 copy-start.2
  347.5 3.5 copy-start.4
  351.0 8.2 %copy-start.9 = (f32[768]{0:T(1024)S(1)}, f32[768]{0:T(1024)}, u32[]{:S(2)}) copy-start(f32[768]{0:T(1024)} %param.36) | copy-start | bytes 9220
  359.2 3.5 copy-start.11
  359.2 14.0 %copy-start.1 = (bf16[768,1536]{1,0:T(8,128)(2,1)S(1)}, bf16[768,1536]{1,0:T(8,128)(2,1)}, u32[]{:S(2)}) copy-start(bf16[768,1536]{1,0:T(8,128)(2,1)} %param.33) | copy-start | bytes 7077892
  362.6 0.9 copy-start.7
  363.6 9.6 %copy-start.8 = (bf16[2,48,768]{2,1,0:T(8,128)(2,1)}, bf16[2,48,768]{2,1,0:T(8,128)(2,1)S(1)}, u32[]{:S(2)}) copy-start(bf16[2,48,768]{2,1,0:T(8,128)(2,1)S(1)} %fusion.30) | copy-start | bytes 442372
  363.8 8.4 %collective-permute-start.3 = (bf16[2,128]{1,0:T(2,128)(2,1)S(1)}, bf16[2,128]{1,0:T(2,128)(2,1)S(1)}, u32[]{:S(2)}, u32[]{:S(2)}) collective-permute-start(bf16[2,128]{1,0:T(2,128)(2,1)S(1)} %bitcast.104), channel_id=1, source_target_pairs={{0,1},{1,2},{2,3},{3,4},{4,5},{5,6},{6,7},{7,8},{8,9},{9,10},{10,1... | collective-permute-start | bytes 1544 | tf_op jit(solution)/shard_map/ppermute | solution.py:36
Sparse Core Ops, SparseCore 0:
  19.7 41.0 all-gather.4
  62.6 215.2 all-gather.2
where the time goes:
time: 382 us; the launch traced here: 380 us
  waiting for transfers between devices  217 us (57%)
  local copies, waits for them, and re-layouts  81.8 us (21%)
  matrix products  32.4 us (8%)
  other arithmetic  17.7 us (5%)
  starting transfers between devices  17.1 us (4%)
  between operations  14.4 us (4%)
    all_gather x1, waiting for transfers between devices, per_device(): lax.all_gather(token_keyvals, 'seq', axis=1, tiled=True)  209 us
    slice x2, local copies, waits for them, and re-layouts, attend(): keyval_piece[:, :, 0]  41.9 us
    unnamed x34, local copies, waits for them, and re-layouts  31.2 us
    dot_general x9, matrix products, project(): jnp.einsum('sac,cd->sad', values, weight, preferred_element_type=jnp.floa...  11.4 us
    ppermute x2, starting transfers between devices, passed_along(): return lax.ppermute(value, axis, pairs)  8.56 us
    dot_general x1, matrix products, per_device(): jnp.einsum('shqd,hde->sqe', attended_tokens, token_output.reshape(HEADS,...  7.96 us
  transfers between devices with their start and end apart: 6, of which 4 were waited for; matrix products, arithmetic and copies ran while one was open for 11% of the time, Pallas kernels for 0%

commit v1 on v0

--- a/solution.py
+++ b/solution.py
@@ -169,7 +169,11 @@
         .reshape(samples, token_rows, 2, model_width)
     )
     best_score, row_total, value_sum = attend(
-        initial, lax.all_gather(token_keyvals, "seq", axis=1, tiled=True), jnp.int32(0)
+        initial,
+        jnp.concatenate(
+            lax.all_to_all(jnp.stack([token_keyvals] * lax.axis_size("seq")), "seq", 0, 0), axis=1
+        ),
+        jnp.int32(0),
     )
     attended_tokens = (value_sum / row_total[..., None]).astype(jnp.bfloat16)
     merged = jnp.einsum(

time: 382 us -> 309 us (0.81)
  waiting for transfers between devices: 217 us -> 162 us
  local copies, waits for them, and re-layouts: 81.8 us -> 48.3 us
  starting transfers between devices: 17.1 us -> 23.5 us
    all_gather x1 -> x0, waiting for transfers between devices: 209 us -> none  [per_device(): lax.all_gather(token_keyvals, 'seq', axis=1, tiled=True)]
    all_to_all x0 -> x1, waiting for transfers between devices: none -> 102 us  [per_device(): lax.all_to_all(jnp.stack([token_keyvals] * lax.axis_size('seq')), 'seq',...]
    all_gather x1, waiting for transfers between devices: 0.02 us -> 51 us  [per_device(): all_bias = lax.all_gather(pair_bias, 'samp', axis=0, tiled=True)]
    slice x2, local copies, waits for them, and re-layouts: 41.9 us -> 14.6 us  [attend(): keyval_piece[:, :, 0]]
    unnamed x34 -> x29, local copies, waits for them, and re-layouts: 31.2 us -> 7.33 us
    all_to_all x0 -> x1, starting transfers between devices: none -> 8.97 us  [per_device(): lax.all_to_all(jnp.stack([token_keyvals] * lax.axis_size('seq')), 'seq',...]
    all_to_all x0 -> x1, local copies, waits for them, and re-layouts: none -> 8.12 us  [per_device(): lax.all_to_all(jnp.stack([token_keyvals] * lax.axis_size('seq')), 'seq',...]
    slice x0 -> x1, local copies, waits for them, and re-layouts: none -> 6.65 us  [attend(): keyval_piece[:, :, 1]]
  transfers between devices with their start and end apart: 6 -> 6, of which waited for: 4 -> 4; matrix products, arithmetic and copies ran while one was open for 11% -> 4% of each run, Pallas kernels for 0% -> 0%
where the time goes in v1:
time: 309 us; the launch traced here: 304 us
  waiting for transfers between devices  162 us (52%)
  local copies, waits for them, and re-layouts  48.3 us (16%)
  matrix products  34.8 us (11%)
  starting transfers between devices  23.5 us (8%)
  other arithmetic  21 us (7%)
  between operations  14.4 us (5%)
    all_to_all x1, waiting for transfers between devices, per_device(): lax.all_to_all(jnp.stack([token_keyvals] * lax.axis_size('seq')), 'seq',...  102 us
    all_gather x1, waiting for transfers between devices, per_device(): all_bias = lax.all_gather(pair_bias, 'samp', axis=0, tiled=True)  51 us
    slice x2, local copies, waits for them, and re-layouts, attend(): keyval_piece[:, :, 0]  14.6 us
    dot_general x9, matrix products, project(): jnp.einsum('sac,cd->sad', values, weight, preferred_element_type=jnp.floa...  10.1 us
    all_to_all x1, starting transfers between devices, per_device(): lax.all_to_all(jnp.stack([token_keyvals] * lax.axis_size('seq')), 'seq',...  8.97 us
    dot_general x1, matrix products, attend(): jnp.einsum('sqhd,skhd->shqk', query_heads, key_heads, preferred_element_t...  8.86 us
    ppermute x2, waiting for transfers between devices, passed_along(): return lax.ppermute(value, axis, pairs)  8.16 us
    all_to_all x1, local copies, waits for them, and re-layouts, per_device(): lax.all_to_all(jnp.stack([token_keyvals] * lax.axis_size('seq')), 'seq',...  8.12 us
  transfers between devices with their start and end apart: 6, of which 4 were waited for; matrix products, arithmetic and copies ran while one was open for 4% of the time, Pallas kernels for 0%

profile of v1, /device:TPU:6, one launch (start us, length us, event | category | flops | bytes accessed | tf_op | source)
XLA Modules:
  0.0 303.9 jit_solution(11870319395494021159)
XLA Ops:
  7.2 1.2 convert_reduce_fusion
  9.7 1.3 convolution_convert_fusion.1
  11.0 3.8 %collective-permute-start = (bf16[2,48,256]{2,1,0:T(8,128)(2,1)S(1)}, bf16[2,48,256]{2,1,0:T(8,128)(2,1)S(1)}, u32[]{:S(2)}, u32[]{:S(2)}) collective-permute-start(bf16[2,48,256]{2,1,0:T(8,128)(2,1)S(1)} %get-tuple-element.26), channel_id=1, source_target_pairs={{0,1},{1,2},{2,3},{3,4},{4,5},{5,6},{6,7},{7,8},{8,9},{9,10},{10,1... | collective-permute-start | bytes 147464 | tf_op jit(solution)/shard_map/ppermute | solution.py:24
  14.9 5.0 %collective-permute-start.1 = (bf16[2,48,256]{2,1,0:T(8,128)(2,1)S(1)}, bf16[2,48,256]{2,1,0:T(8,128)(2,1)S(1)}, u32[]{:S(2)}, u32[]{:S(2)}) collective-permute-start(bf16[2,48,256]{2,1,0:T(8,128)(2,1)S(1)} %get-tuple-element.27), channel_id=1, source_target_pairs={{1,0},{2,1},{3,2},{4,3},{5,4},{6,5},{7,6},{8,7},{9,8},{10,9},{11,1... | collective-permute-start | bytes 147464 | tf_op jit(solution)/shard_map/ppermute | solution.py:26
  20.7 1.3 convolution_convert_fusion.2
  26.7 2.4 copy.79
  29.0 1.5 copy.81
  30.6 1.5 copy.80
  32.1 1.5 copy.82
  33.5 4.8 %pad_maximum_fusion = bf16[2,12,128,256]{2,3,1,0:T(8,128)(2,1)S(1)} fusion(bf16[2,12,32,256]{2,3,1,0:T(8,128)(2,1)} %copy.82, bf16[2,12,32,256]{2,3,1,0:T(8,128)(2,1)} %copy.81, bf16[2,12,32,256]{2,3,1,0:T(8,128)(2,1)} %copy.80, bf16[2,12,32,256]{2,3,1,0:T(8,128)(2,1)} %copy.79), kind=kLoop, calls=%fused_computation.19 | loop fusion | flops 6291456 | bytes 3145728 | tf_op jit(solution)/shard_map/concatenate | solution.py:120
  38.4 1.3 fusion.96
  39.7 3.2 %fusion.99 = (f32[2,4,12,32]{3,2,1,0:T(8,128)S(1)}, f32[2,4,12,32,128]{4,3,2,1,0:T(8,128)}) fusion(bf16[2,12,128,4,32]{2,4,3,1,0:T(8,128)(2,1)} %bitcast.110, bf16[2,12,32,4,32]{4,3,2,1,0:T(4,128)(2,1)} %reshape.173, f32[4,12,32,128]{3,2,1,0:T(8,128)S(1)} %copy-done.5, pred[12,128]{1,0:T(8,128)(4,1)S(1)} %fusion.89), kind=kOutput, calls=%fused_computation.118 | convolution fusion | flops 27132032 | bytes 3356160 | tf_op jit(solution)/shard_map/sub | solution.py:48
  42.9 3.2 %fusion.20 = bf16[2,12,32,4,32]{2,4,3,1,0:T(8,128)(2,1)} fusion(bf16[2,12,128,4,32]{2,4,3,1,0:T(8,128)(2,1)} %bitcast.109, f32[2,4,12,32,128]{4,3,2,1,0:T(8,128)} %get-tuple-element.31, f32[2,4,12,32]{3,2,1,0:T(8,128)S(1)} %get-tuple-element.30), kind=kOutput, calls=%fused_computation.24 | convolution fusion | flops 26050560 | bytes 2568192 | tf_op jit(solution)/shard_map/shwqk,swkhd->swqhd/dot_general | solution.py:135
  46.1 1.5 copy.65
  49.0 1.4 maximum_convert_fusion
  50.7 3.5 %collective-permute-start.2 = (f32[2,768]{1,0:T(2,128)S(1)}, f32[2,768]{1,0:T(2,128)S(1)}, u32[]{:S(2)}, u32[]{:S(2)}) collective-permute-start(f32[2,768]{1,0:T(2,128)S(1)} %bitcast.111), channel_id=1, source_target_pairs={{1,0},{2,1},{3,2},{4,3},{5,4},{6,5},{7,6},{8,7},{9,8},{10,9},{11,1... | collective-permute-start | bytes 18440 | tf_op jit(solution)/shard_map/ppermute | solution.py:36
  54.6 1.7 collective-permute-done.2
  57.3 4.7 %stack.3 = bf16[32,2,48,2,768]{4,2,3,1,0:T(8,128)(2,1)} broadcast(bf16[2,48,2,768]{3,1,2,0:T(8,128)(2,1)S(1)} %bitcast.107), dimensions={1,2,3,4} | broadcast | bytes 9732096 | tf_op jit(solution)/shard_map/stack | solution.py:174
  62.1 9.0 %all-to-all-start = ((bf16[32,2,48,2,768]{4,2,3,1,0:T(8,128)(2,1)}), bf16[32,2,48,2,768]{4,2,3,1,0:T(8,128)(2,1)}, u32[]{:S(2)}, u32[]{:S(2)}) async-start(bf16[32,2,48,2,768]{4,2,3,1,0:T(8,128)(2,1)} %stack.3), calls=%async_computation | async-start | bytes 18874368 | tf_op jit(solution)/shard_map/all_to_all | solution.py:174
  72.6 51.0 %all-gather.2.cloned.1.call-done = bf16[16,48,1536]{2,1,0:T(8,128)(2,1)} async-done(((bf16[2,48,1536]{2,1,0:T(8,128)(2,1)}), bf16[16,48,1536]{2,1,0:T(8,128)(2,1)}) %all-gather.2.cloned.1.call-update) | async-done | bytes 2359312 | tf_op jit(solution)/shard_map/all_gather | solution.py:162
  123.7 4.4 %convert_element_type.104 = f32[16,48,1536]{2,1,0:T(8,128)} convert(bf16[16,48,1536]{2,1,0:T(8,128)(2,1)} %all-gather.2.cloned.1.call-done) | non-fusion elementwise | flops 1179648 | bytes 7077888 | tf_op jit(solution)/shard_map/convert_element_type | solution.py:67
  128.1 102.2 %all-to-all-done = bf16[32,2,48,2,768]{4,2,3,1,0:T(8,128)(2,1)} async-done(((bf16[32,2,48,2,768]{4,2,3,1,0:T(8,128)(2,1)}), bf16[32,2,48,2,768]{4,2,3,1,0:T(8,128)(2,1)}, u32[]{:S(2)}, u32[]{:S(2)}) %all-to-all-start) | async-done | bytes 9437216 | tf_op jit(solution)/shard_map/all_to_all | solution.py:174
  230.3 8.1 %copy.68 = bf16[32,2,48,2,768]{4,2,0,3,1:T(8,128)(2,1)} copy(bf16[32,2,48,2,768]{4,2,3,1,0:T(8,128)(2,1)} %all-to-all-done) | data formatting | bytes 18874368 | tf_op jit(solution)/shard_map/all_to_all | solution.py:174
  238.4 7.9 %fusion.95 = (bf16[2,1536,1,768]{3,1,2,0:T(8,128)(2,1)}, bf16[2,1536,1,768]{3,1,2,0:T(8,128)(2,1)}) fusion(bf16[2,1536,2,768]{3,1,2,0:T(8,128)(2,1)} %bitcast.101), kind=kLoop, calls=%fused_computation.114 | loop fusion | bytes 18874368 | tf_op jit(solution)/shard_map/slice | solution.py:62
  246.4 6.7 %copy.69 = bf16[2,1536,1,768]{1,3,0,2:T(8,128)(2,1)} copy(bf16[2,1536,1,768]{3,1,2,0:T(8,128)(2,1)} %get-tuple-element.18) | data formatting | bytes 9437184 | tf_op jit(solution)/shard_map/slice | solution.py:62
  253.0 8.9 %fusion.1 = (f32[2,16,48]{2,1,0:T(8,128)S(1)}, f32[2,16,48,1536]{3,2,1,0:T(8,128)}) fusion(f32[16,48,1536]{2,1,0:T(8,128)} %convert_element_type.104, bf16[2,1536,16,48]{1,3,2,0:T(8,128)(2,1)} %bitcast.102, bf16[2,48,16,48]{3,2,1,0:T(8,128)(2,1)S(1)} %reshape.177), kind=kOutput, calls=%fused_computation.3 | convolution fusion | flops 233568768 | bytes 19027968 | tf_op jit(solution)/shard_map/sqhd,skhd->shqk/dot_general | solution.py:64
  261.9 6.7 %copy.71 = bf16[2,1536,1,768]{1,3,0,2:T(8,128)(2,1)} copy(bf16[2,1536,1,768]{3,1,2,0:T(8,128)(2,1)} %get-tuple-element.19) | data formatting | bytes 9437184 | tf_op jit(solution)/shard_map/slice | solution.py:63
  268.5 6.2 %fusion.2 = f32[2,16,48]{2,1,0:T(8,128)S(1)} fusion(f32[2,16,48,1536]{3,2,1,0:T(8,128)} %get-tuple-element.33, f32[2,16,48]{2,1,0:T(8,128)S(1)} %broadcast_maximum_fusion, f32[16,48,1536]{2,1,0:T(8,128)} %convert_element_type.104), kind=kLoop, calls=%fused_computation.4 | loop fusion | flops 9435648 | bytes 14168064 | tf_op jit(solution)/shard_map/reduce_sum | solution.py:70
  274.8 8.0 %fusion.100 = (f32[2,48]{1,0:T(2,128)S(1)}, f32[2,48,768]{2,1,0:T(8,128)S(1)}) fusion(bf16[16,48,768,1]{2,1,0,3:T(8,128)(2,1)S(1)} %bitcast.106, bf16[2,1536,16,48]{1,3,2,0:T(8,128)(2,1)} %bitcast.103, f32[2,16,48,1536]{3,2,1,0:T(8,128)} %get-tuple-element.33, f32[2,16,48]{2,1,0:T(8,128)S(1)} %broadcast_maximum_fusion, ...), kind=kOutput, calls=%fused_computation.119 | convolution fusion | flops 349691808 | bytes 20509056 | tf_op jit(solution)/shard_map/shqd,hde->sqe/dot_general | solution.py:179
  283.0 3.4 %fusion.6 = f32[2,48,3072]{2,1,0:T(8,128)S(1)} fusion(bf16[768,3072]{1,0:T(8,128)(2,1)} %param.37, f32[2,48,768]{2,1,0:T(8,128)S(1)} %get-tuple-element.35, f32[768]{0:T(1024)S(1)} %copy-done.9, f32[2,48]{1,0:T(2,128)S(1)} %add_rsqrt_fusion.1, f32[2,48]{1,0:T(2,128)S(1)} %broadcast_multiply_fusion.1), kind=kOutput, calls=%fused_computation.7 | convolution fusion | flops 453279744 | bytes 6196992 | tf_op jit(solution)/shard_map/sac,cd->sad/dot_general | solution.py:53
  287.6 1.9 collective-permute-start.3
  289.5 6.5 %collective-permute-done.3 = bf16[2,128]{1,0:T(2,128)(2,1)S(1)} collective-permute-done((bf16[2,128]{1,0:T(2,128)(2,1)S(1)}, bf16[2,128]{1,0:T(2,128)(2,1)S(1)}, u32[]{:S(2)}, u32[]{:S(2)}) %collective-permute-start.3) | collective-permute-done | bytes 544 | tf_op jit(solution)/shard_map/ppermute | solution.py:36
  (70 shorter events, 13.5 us)
Async XLA Ops:
  7.2 49.6 %copy-start = (bf16[768,1536]{1,0:T(8,128)(2,1)S(1)}, bf16[768,1536]{1,0:T(8,128)(2,1)}, u32[]{:S(2)}) copy-start(bf16[768,1536]{1,0:T(8,128)(2,1)} %param.33) | copy-start | bytes 7077892
  7.2 17.5 %copy-start.6 = (bf16[4,12,32,128]{3,2,1,0:T(8,128)(2,1)S(1)}, bf16[4,12,32,128]{3,2,1,0:T(8,128)(2,1)}, u32[]{:S(2)}) copy-start(bf16[4,12,32,128]{3,2,1,0:T(8,128)(2,1)} %param.26) | copy-start | bytes 1179652
  11.0 14.6 %collective-permute-start = (bf16[2,48,256]{2,1,0:T(8,128)(2,1)S(1)}, bf16[2,48,256]{2,1,0:T(8,128)(2,1)S(1)}, u32[]{:S(2)}, u32[]{:S(2)}) collective-permute-start(bf16[2,48,256]{2,1,0:T(8,128)(2,1)S(1)} %get-tuple-element.26), channel_id=1, source_target_pairs={{0,1},{1,2},{2,3},{3,4},{4,5},{5,6},{6,7},{7,8},{8,9},{9,10},{10,1... | collective-permute-start | bytes 147464 | tf_op jit(solution)/shard_map/ppermute | solution.py:24
  14.9 10.8 %collective-permute-start.1 = (bf16[2,48,256]{2,1,0:T(8,128)(2,1)S(1)}, bf16[2,48,256]{2,1,0:T(8,128)(2,1)S(1)}, u32[]{:S(2)}, u32[]{:S(2)}) collective-permute-start(bf16[2,48,256]{2,1,0:T(8,128)(2,1)S(1)} %get-tuple-element.27), channel_id=1, source_target_pairs={{1,0},{2,1},{3,2},{4,3},{5,4},{6,5},{7,6},{8,7},{9,8},{10,9},{11,1... | collective-permute-start | bytes 147464 | tf_op jit(solution)/shard_map/ppermute | solution.py:26
  38.4 1.4 copy-start.5
  46.1 2.0 copy-start.2
  49.0 7.7 %copy-start.10 = (f32[768]{0:T(1024)S(1)}, f32[768]{0:T(1024)}, u32[]{:S(2)}) copy-start(f32[768]{0:T(1024)} %param.31) | copy-start | bytes 9220
  50.7 5.5 %collective-permute-start.2 = (f32[2,768]{1,0:T(2,128)S(1)}, f32[2,768]{1,0:T(2,128)S(1)}, u32[]{:S(2)}, u32[]{:S(2)}) collective-permute-start(f32[2,768]{1,0:T(2,128)S(1)} %bitcast.111), channel_id=1, source_target_pairs={{1,0},{2,1},{3,2},{4,3},{5,4},{6,5},{7,6},{8,7},{9,8},{10,9},{11,1... | collective-permute-start | bytes 18440 | tf_op jit(solution)/shard_map/ppermute | solution.py:36
  62.1 9.7 %copy-start.4 = (bf16[768,768]{1,0:T(8,128)(2,1)S(1)}, bf16[768,768]{1,0:T(8,128)(2,1)}, u32[]{:S(2)}) copy-start(bf16[768,768]{1,0:T(8,128)(2,1)} %param.32) | copy-start | bytes 3538948
  62.1 168.2 %all-to-all-start = ((bf16[32,2,48,2,768]{4,2,3,1,0:T(8,128)(2,1)}), bf16[32,2,48,2,768]{4,2,3,1,0:T(8,128)(2,1)}, u32[]{:S(2)}, u32[]{:S(2)}) async-start(bf16[32,2,48,2,768]{4,2,3,1,0:T(8,128)(2,1)} %stack.3), calls=%async_computation | async-start | bytes 18874368 | tf_op jit(solution)/shard_map/all_to_all | solution.py:174
  71.0 52.6 %all-gather.2.cloned.1.call-start = ((), (), s32[]{:S(2)}) async-start(), calls=%async_computation.1 | async-start | bytes 2654208 | tf_op jit(solution)/shard_map/all_gather | solution.py:162
  268.5 6.2 %copy-start.3 = (bf16[768,768]{1,0:T(8,128)(2,1)S(1)}, bf16[768,768]{1,0:T(8,128)(2,1)}, u32[]{:S(2)}) copy-start(bf16[768,768]{1,0:T(8,128)(2,1)} %param.34) | copy-start | bytes 3538948
  274.8 8.2 %copy-start.9 = (f32[768]{0:T(1024)S(1)}, f32[768]{0:T(1024)}, u32[]{:S(2)}) copy-start(f32[768]{0:T(1024)} %param.36) | copy-start | bytes 9220
  283.0 3.5 %copy-start.11 = (bf16[1536,768]{1,0:T(8,128)(2,1)S(1)}, bf16[1536,768]{1,0:T(8,128)(2,1)}, u32[]{:S(2)}) copy-start(bf16[1536,768]{1,0:T(8,128)(2,1)} %param.38) | copy-start | bytes 7077892
  283.0 14.0 %copy-start.1 = (bf16[768,1536]{1,0:T(8,128)(2,1)S(1)}, bf16[768,1536]{1,0:T(8,128)(2,1)}, u32[]{:S(2)}) copy-start(bf16[768,1536]{1,0:T(8,128)(2,1)} %param.33) | copy-start | bytes 7077892
  286.5 0.9 copy-start.7
  287.4 9.6 %copy-start.8 = (bf16[2,48,768]{2,1,0:T(8,128)(2,1)}, bf16[2,48,768]{2,1,0:T(8,128)(2,1)S(1)}, u32[]{:S(2)}) copy-start(bf16[2,48,768]{2,1,0:T(8,128)(2,1)S(1)} %fusion.30) | copy-start | bytes 442372
  287.6 8.4 %collective-permute-start.3 = (bf16[2,128]{1,0:T(2,128)(2,1)S(1)}, bf16[2,128]{1,0:T(2,128)(2,1)S(1)}, u32[]{:S(2)}, u32[]{:S(2)}) collective-permute-start(bf16[2,128]{1,0:T(2,128)(2,1)S(1)} %bitcast.112), channel_id=1, source_target_pairs={{0,1},{1,2},{2,3},{3,4},{4,5},{5,6},{6,7},{7,8},{8,9},{9,10},{10,1... | collective-permute-start | bytes 1544 | tf_op jit(solution)/shard_map/ppermute | solution.py:36
Sparse Core Ops, SparseCore 0:
  73.7 49.9 all-gather.1
